TPU v7x, 32 devices: a whole 2x2x4 slice. The times are simulated.
32 devices in a mesh: sect: 4 (over y, x), blk: 8 (over z, core).
Axes of the slice: x: 2, y: 2, z: 4, core: 2. Of those that a mesh axis runs over, the one named last changes fastest.
Arguments:
- queries: bfloat16 [1024, 4096], P('blk', 'sect'), may hold values from -512 to 512
- kv_cache: bfloat16 [1024, 32, 2048], P('blk', None, 'sect'), may hold values from -6 to 6
- lengths: int32 [1024], P('blk'), may hold values from 1 to 32, 16384 in all
- resid_in: bfloat16 [1024, 4096], P('blk', 'sect'), may hold values from -10 to 10
- norm_gain: float32 [4096], replicated, may hold values from 0.1 to 1.9
- w_gate: bfloat16 [4096, 14336], P(None, 'blk'), may hold values from -0.09375 to 0.09375
- w_up: bfloat16 [4096, 14336], P(None, 'blk'), may hold values from -0.09375 to 0.09375
- w_down: bfloat16 [14336, 4096], P('blk'), may hold values from -0.046875 to 0.046875
Outputs:
- layer_out: bfloat16 [1024, 4096], P('blk', 'sect')
Inputs may be any that keep to these rules, and one draw needn't show every extreme that they name: `lengths`: each row has 1 to 32 live slots and some row has exactly 32.
All inputs are finite; a program needn't handle non-finite values. No bound on the sum of `lengths` on one device may be relied on, other than what follows from the above.
Results may differ from a plain program's by a relative error of at most 0.0068.
Values may be sent and summed in bfloat16 or wider, within the bound.
A program may use at most 128 MiB of HBM per device.

v0:
```python
import jax
import jax.numpy as jnp
from jax import lax
from jax.sharding import PartitionSpec as P

HD = 128
GROUP = 4


def attention(queries, kv_cache, lengths):
    rows = queries.shape[0]
    slots = kv_cache.shape[1]
    heads_kv = kv_cache.shape[2] // (2 * HD)
    query = queries.reshape(rows, heads_kv, GROUP, HD)
    cache = kv_cache.reshape(rows, slots, heads_kv, 2, HD)
    keys = cache[:, :, :, 0, :]
    values = cache[:, :, :, 1, :]
    scores = jnp.einsum("rkgd,rlkd->rkgl", query, keys, preferred_element_type=jnp.float32)
    scores = scores / jnp.sqrt(jnp.float32(HD))
    positions = jnp.arange(slots, dtype=jnp.int32)
    live = positions[None, None, None, :] < lengths[:, None, None, None]
    scores = jnp.where(live, scores, jnp.float32(-1e30))
    top = jnp.max(scores, axis=-1, keepdims=True)
    expo = jnp.where(live, jnp.exp(scores - top), jnp.float32(0.0))
    probs = (expo / jnp.sum(expo, axis=-1, keepdims=True)).astype(jnp.bfloat16)
    attn = jnp.einsum("rkgl,rlkd->rkgd", probs, values, preferred_element_type=jnp.float32)
    return attn.reshape(rows, heads_kv * GROUP * HD)


def feed_forward(normed, w_gate, w_up, w_down):
    piece = lax.all_gather(normed, "blk", axis=0, tiled=True)
    gate = jnp.dot(piece, w_gate, preferred_element_type=jnp.float32)
    upval = jnp.dot(piece, w_up, preferred_element_type=jnp.float32)
    act = (jax.nn.silu(gate) * upval).astype(jnp.bfloat16)
    return lax.psum_scatter(
        jnp.dot(act, w_down, preferred_element_type=jnp.float32),
        "blk",
        scatter_dimension=0,
        tiled=True,
    )


def body(queries, kv_cache, lengths, resid_in, norm_gain, w_gate, w_up, w_down):
    attn = attention(queries, kv_cache, lengths)
    hidden_state = (resid_in.astype(jnp.float32) + attn).astype(jnp.bfloat16)
    row_state = lax.all_to_all(
        hidden_state, "sect", split_axis=0, concat_axis=1, tiled=True
    ).astype(jnp.float32)
    meansq = jnp.mean(row_state * row_state, axis=1, keepdims=True)
    normed = (row_state * lax.rsqrt(meansq + 1e-05) * norm_gain[None, :]).astype(jnp.bfloat16)
    ffn_out = feed_forward(normed, w_gate, w_up, w_down)
    finished = (row_state + ffn_out).astype(jnp.bfloat16)
    return lax.all_to_all(finished, "sect", split_axis=1, concat_axis=0, tiled=True)


def solution(mesh):
    placed = (
        P("blk", "sect"),
        P("blk", None, "sect"),
        P("blk"),
        P("blk", "sect"),
        P(),
        P(None, "blk"),
        P(None, "blk"),
        P("blk", None),
    )
    return jax.shard_map(
        body, mesh=mesh, in_specs=placed, out_specs=P("blk", "sect"), check_vma=False
    )
```

profile of v0, /device:TPU:0, one launch (start us, length us, event | category | flops | bytes accessed | tf_op | source)
XLA Modules:
  0.0 170.2 jit_solution(17144635806944393871)
XLA Ops:
  6.5 0.0 all-gather.2.cloned.1.call-start
  6.5 7.9 %copy.16 = bf16[128,32,512]{0,2,1:T(8,128)(2,1)} copy(bf16[128,32,512]{2,1,0:T(8,128)(2,1)} %param.9) | data formatting | bytes 8388608 | tf_op args[1]
  14.4 4.0 %fusion.19 = (bf16[128,32,2,1,128]{0,4,3,2,1:T(8,128)(2,1)}, bf16[128,32,2,1,128]{0,4,3,2,1:T(8,128)(2,1)S(1)}) fusion(bf16[128,32,2,2,128]{0,4,3,2,1:T(8,128)(2,1)} %bitcast.31), kind=kLoop, calls=%fused_computation.25 | loop fusion | bytes 8388608 | tf_op jit(solution)/shard_map/slice | solution.py:16
  18.4 0.0 copy-start.1
  18.4 0.0 copy-start.4
  18.4 4.6 %copy.21 = bf16[128,32,2,1,128]{4,1,2,0,3:T(8,128)(2,1)} copy(bf16[128,32,2,1,128]{0,4,3,2,1:T(8,128)(2,1)} %get-tuple-element.5) | data formatting | bytes 4194304
  23.1 0.0 copy-done.1
  23.1 0.2 reshape.49
  23.3 0.0 copy-done.4
  23.3 0.1 iota_compare_fusion
  23.4 3.0 %copy.22 = bf16[128,32,2,1,128]{4,1,2,0,3:T(8,128)(2,1)} copy(bf16[128,32,2,1,128]{0,4,3,2,1:T(8,128)(2,1)S(1)} %get-tuple-element.6) | data formatting | bytes 4194304
  26.3 0.0 copy-start
  26.3 3.2 %fusion.20 = (f32[128,2,4]{2,1,0:T(2,128)S(1)}, f32[128,2,4,32]{3,2,1,0:T(4,128)S(1)}) fusion(pred[128,32]{1,0:T(8,128)(4,1)S(1)} %iota_compare_fusion, bf16[128,2,4,128]{3,2,1,0:T(4,128)(2,1)S(1)} %reshape.49, bf16[128,32,2,1,128]{4,1,2,0,3:T(8,128)(2,1)} %copy.21), kind=kOutput, calls=%fused_computation.26 | convolution fusion | flops 8552479 | bytes 2498560 | tf_op jit(solution)/shard_map/sub | solution.py:24
  29.5 0.0 copy-done
  29.5 0.0 copy-start.2
  29.5 0.7 fusion.2
  30.2 0.2 reshape.51
  30.5 0.0 copy-done.2
  30.5 0.0 copy-start.3
  30.5 0.1 add_convert_fusion.1
  30.5 10.7 %all_to_all.32 = bf16[4,32,1024]{2,1,0:T(8,128)(2,1)S(1)} all-to-all(bf16[4,32,1024]{2,1,0:T(8,128)(2,1)S(1)} %bitcast.37), channel_id=1, replica_groups=mesh['sect'=4,'blk'=8] {'sect'}, dimensions={0} | all-to-all | bytes 524288 | tf_op jit(solution)/shard_map/all_to_all | solution.py:46
  41.3 0.2 fusion.16
  41.5 0.0 copy-done.3
  41.5 0.8 multiply_convert_fusion
  42.3 0.0 all-gather.2.cloned.1.call-update
  42.4 0.2 reduce-scatter.2.cloned.1.call-start
  42.6 28.7 %all-gather.2.cloned.1.call-done = bf16[256,4096]{1,0:T(8,128)(2,1)} async-done(((bf16[32,4096]{1,0:T(8,128)(2,1)}), bf16[256,4096]{1,0:T(8,128)(2,1)}) %all-gather.2.cloned.1.call-update) | async-done | bytes 2097168 | tf_op jit(solution)/shard_map/all_gather | solution.py:31
  71.3 0.0 copy-start.5
  71.3 11.2 %fusion.23 = f32[256,1792]{1,0:T(8,128)} fusion(bf16[256,4096]{1,0:T(8,128)(2,1)} %all-gather.2.cloned.1.call-done, bf16[4096,1792]{1,0:T(8,128)(2,1)} %param.13), kind=kOutput, calls=%fused_computation.27 | convolution fusion | flops 3758096384 | bytes 18612224 | tf_op jit(solution)/shard_map/dot_general | solution.py:32
  82.5 0.0 copy-done.5
  82.5 20.2 %fusion.15 = f32[256,4096]{1,0:T(8,128)} fusion(bf16[1792,4096]{1,0:T(8,128)(2,1)} %param.15, bf16[256,4096]{1,0:T(8,128)(2,1)S(1)} %copy-done.5, bf16[4096,1792]{1,0:T(8,128)(2,1)} %param.14, f32[256,1792]{1,0:T(8,128)} %fusion.23), kind=kOutput, calls=%fused_computation.12 | convolution fusion | flops 7518945280 | bytes 37486592 | tf_op jit(solution)/shard_map/dot_general | solution.py:36
  102.7 0.0 reduce-scatter.2.cloned.1.call-update
  102.7 49.7 %reduce-scatter.2.cloned.1.call-done = f32[32,4096]{1,0:T(8,128)} async-done(((f32[256,4096]{1,0:T(8,128)}), f32[32,4096]{1,0:T(8,128)}) %reduce-scatter.2.cloned.1.call-update) | async-done | bytes 524304 | tf_op jit(solution)/shard_map/reduce_scatter | solution.py:35
  152.4 1.1 add_convert_fusion
  153.5 9.2 %all_to_all.33 = bf16[32,4,1024]{2,0,1:T(8,128)(2,1)S(1)} all-to-all(bf16[32,4,1024]{2,0,1:T(8,128)(2,1)S(1)} %bitcast.35), channel_id=1, replica_groups=mesh['sect'=4,'blk'=8] {'sect'}, dimensions={1} | all-to-all | bytes 524288 | tf_op jit(solution)/shard_map/all_to_all | solution.py:53
  162.7 0.7 copy.28
  (4 shorter events, 0.1 us)
Async XLA Ops:
  6.5 64.8 %all-gather.2.cloned.1.call-start = ((), (), s32[]{:S(2)}) async-start(), calls=%async_computation.3 | async-start | bytes 2359296 | tf_op jit(solution)/shard_map/all_gather | solution.py:31
  18.4 4.6 %copy-start.1 = (bf16[128,1024]{1,0:T(8,128)(2,1)S(1)}, bf16[128,1024]{1,0:T(8,128)(2,1)}, u32[]{:S(2)}) copy-start(bf16[128,1024]{1,0:T(8,128)(2,1)} %param.8) | copy-start | bytes 786436
  18.4 4.8 %copy-start.4 = (s32[128]{0:T(128)S(1)}, s32[128]{0:T(128)}, u32[]{:S(2)}) copy-start(s32[128]{0:T(128)} %param.10) | copy-start | bytes 1540
  26.3 3.2 %copy-start = (bf16[128,32,2,1,128]{4,1,2,0,3:T(8,128)(2,1)S(1)}, bf16[128,32,2,1,128]{4,1,2,0,3:T(8,128)(2,1)}, u32[]{:S(2)}) copy-start(bf16[128,32,2,1,128]{4,1,2,0,3:T(8,128)(2,1)} %copy.22) | copy-start | bytes 6291460
  29.5 1.0 copy-start.2
  30.5 11.0 %copy-start.3 = (f32[4096]{0:T(1024)S(1)}, f32[4096]{0:T(1024)}, u32[]{:S(2)}) copy-start(f32[4096]{0:T(1024)} %param.12) | copy-start | bytes 49156
  42.4 110.0 %reduce-scatter.2.cloned.1.call-start = ((), (), s32[]{:S(2)}) async-start(), calls=%async_computation.4 | async-start | bytes 4718592 | tf_op jit(solution)/shard_map/reduce_scatter | solution.py:35
  71.3 11.2 %copy-start.5 = (bf16[256,4096]{1,0:T(8,128)(2,1)S(1)}, bf16[256,4096]{1,0:T(8,128)(2,1)}, u32[]{:S(2)}) copy-start(bf16[256,4096]{1,0:T(8,128)(2,1)} %all-gather.2.cloned.1.call-done) | copy-start | bytes 6291460
Sparse Core Ops, SparseCore 0:
  42.5 28.8 all-gather.1
  102.8 49.4 reduce-scatter.1
where the time goes:
time: 171 us; the launch traced here: 170 us
  waiting for transfers between devices  78.4 us (46%)
  matrix products  35.2 us (21%)
  local copies, waits for them, and re-layouts  20.7 us (12%)
  blocking collectives  19.9 us (12%)
  between operations  13.5 us (8%)
  other arithmetic  2.27 us (1%)
    reduce_scatter x1, waiting for transfers between devices, feed_forward(): lax.psum_scatter(jnp.dot(act, w_down, preferred_element_type=jnp.float32)...  49.7 us
    all_gather x1, waiting for transfers between devices, feed_forward(): piece = lax.all_gather(normed, 'blk', axis=0, tiled=True)  28.7 us
    dot_general x1, matrix products, feed_forward(): jnp.dot(act, w_down, preferred_element_type=jnp.float32)  20.2 us
    unnamed x16, local copies, waits for them, and re-layouts  16.2 us
    dot_general x1, matrix products, feed_forward(): gate = jnp.dot(piece, w_gate, preferred_element_type=jnp.float32)  11.2 us
    all_to_all x1, blocking collectives, body(): lax.all_to_all(hidden_state, 'sect', split_axis=0, concat_axis=1, tiled=T...  10.7 us
    all_to_all x1, blocking collectives, body(): lax.all_to_all(finished, 'sect', split_axis=1, concat_axis=0, tiled=True)  9.17 us
    slice x1, local copies, waits for them, and re-layouts, attention(): keys = cache[:, :, :, 0, :]  4 us
  transfers between devices with their start and end apart: 2, of which 2 were waited for; matrix products, arithmetic and copies ran while one was open for 0% of the time, Pallas kernels for 0%

commit v1 on v0

v1 whole, which is shorter than its diff:
```python
import functools

import jax
import jax.numpy as jnp
from jax import lax
from jax.experimental import pallas as pl
from jax.experimental.pallas import tpu as pltpu
from jax.sharding import PartitionSpec as P

HD = 128
GROUP = 4
TILE = 16
MESH = pl.DeviceIdType.MESH
F32 = jnp.float32
BF16 = jnp.bfloat16


def kernel(
    S, C,
    q_ref, kv_hbm, len_ref, resid_ref, gain_ref, wg_hbm, wu_hbm, wd_hbm,
    out_ref,
    wg, wu, wd, hb, rs, xs, ss, sr, sb, ru, rd, own, fo, ob,
    kv_sem, w_sem, a_send, a_recv, x_send, x_recv, s_send, s_recv,
    l_send, u_recv, d_recv, o_send, o_recv,
):
    RS = rs.shape[1]
    KC = rs.shape[2]
    B = 2 * C
    FFL = wg.shape[2]
    heads = kv_hbm.shape[2] // (2 * HD)
    slots = kv_hbm.shape[1]
    NT = 256 if FFL % 256 == 0 else 128
    NK = 256 if KC % 256 == 0 else 128

    sect = lax.axis_index("sect")
    blk = lax.axis_index("blk")
    chip = blk // 2
    core = blk % 2
    sib = chip * 2 + (1 - core)
    up = blk + 2
    down = blk - 2
    has_up = chip < C - 1
    has_down = chip > 0
    me = core * C + chip

    def order(i):
        return lax.rem(sect + 1 + i, S)

    def remote(src, dst, ssem, rsem, dev):
        return pltpu.make_async_remote_copy(
            src_ref=src, dst_ref=dst, send_sem=ssem, recv_sem=rsem,
            device_id=dev, device_id_type=MESH,
        )

    def weight_copy(i, w):
        t = order(i)
        rows = pl.ds(pl.multiple_of(t * KC, KC), KC)
        src = (wg_hbm.at[rows, :], wu_hbm.at[rows, :], wd_hbm.at[:, rows])[w]
        return pltpu.make_async_copy(src, (wg, wu, wd)[w].at[t], w_sem.at[w, t])

    def greet():
        barrier = pltpu.get_barrier_semaphore()
        for e in range(1, S):
            pl.semaphore_signal(
                barrier, inc=1, device_id={"sect": lax.rem(sect + e, S)}, device_id_type=MESH
            )
        pl.semaphore_signal(barrier, inc=1, device_id={"blk": sib}, device_id_type=MESH)

        @pl.when(has_up)
        def _():
            pl.semaphore_signal(barrier, inc=1, device_id={"blk": up}, device_id_type=MESH)

        @pl.when(has_down)
        def _():
            pl.semaphore_signal(barrier, inc=1, device_id={"blk": down}, device_id_type=MESH)

        pl.semaphore_wait(barrier, S + has_up.astype(jnp.int32) + has_down.astype(jnp.int32))

    def a_copy(t):
        return remote(hb.at[t], rs.at[sect], a_send.at[t], a_recv.at[sect], {"sect": t})

    def a_wait(t):
        remote(hb.at[t], rs.at[t], a_send.at[t], a_recv.at[t], {"sect": t}).wait_recv()

    def front(kv):
        def kv_copy(t):
            rows = pl.ds(pl.multiple_of(t * RS, RS), RS)
            return pltpu.make_async_copy(kv_hbm.at[rows], kv.at[t], kv_sem.at[t])

        for i in range(S):
            kv_copy(order(i)).start()
        for i in range(S):
            weight_copy(i, 0).start()
            weight_copy(i, 1).start()
        for i in range(S):
            weight_copy(i, 2).start()

        def attend(t, dst, slot):
            kv_copy(t).wait()
            for g in range(RS // TILE):
                rows = pl.ds(pl.multiple_of(t * RS + g * TILE, TILE), TILE)
                count = jnp.concatenate([len_ref[rows, :]] * GROUP, axis=0)
                shape = (GROUP * TILE, TILE * slots)
                row = lax.rem(lax.broadcasted_iota(jnp.int32, shape, 0), TILE)
                col = lax.broadcasted_iota(jnp.int32, shape, 1) - row * slots
                live = (col >= 0) & (col < count)
                for h in range(heads):
                    base = h * GROUP * HD
                    query = jnp.concatenate(
                        [q_ref[rows, base + e * HD:base + (e + 1) * HD] for e in range(GROUP)], axis=0
                    )
                    part = kv[t, g * TILE:(g + 1) * TILE, :, h * 2 * HD:(h + 1) * 2 * HD]
                    part = part.reshape(TILE * slots, 2 * HD)
                    scores = lax.dot_general(
                        query, part[:, :HD], (((1,), (1,)), ((), ())), preferred_element_type=F32
                    ) * (HD ** -0.5)
                    scores = jnp.where(live, scores, -1e30)
                    top = jnp.max(scores, axis=1, keepdims=True)
                    expo = jnp.where(live, jnp.exp(scores - top), 0.0)
                    probs = (expo / jnp.sum(expo, axis=1, keepdims=True)).astype(BF16)
                    attn = jnp.dot(probs, part[:, HD:], preferred_element_type=F32)
                    for e in range(GROUP):
                        cols = slice(base + e * HD, base + (e + 1) * HD)
                        dst[slot, g * TILE:(g + 1) * TILE, cols] = (
                            resid_ref[rows, cols].astype(F32) + attn[e * TILE:(e + 1) * TILE]
                        ).astype(BF16)

        greet()

        @pl.loop(0, S - 1)
        def _(i):
            t = order(i)
            attend(t, hb, t)
            a_copy(t).start()

        attend(sect, rs, sect)

    pl.run_scoped(front, pltpu.VMEM((S, RS, slots, kv_hbm.shape[2]), BF16))

    def x_line(j, c, which):
        slot = core * C + c
        return remote(
            xs.at[j, slot], xs.at[j, slot], x_send.at[j, c, which], x_recv.at[j, slot],
            {"blk": up if which == 0 else down},
        )

    def x_sib(j, c):
        slot = core * C + c
        return remote(
            xs.at[j, slot], xs.at[j, slot], x_send.at[j, c, 2], x_recv.at[j, slot], {"blk": sib}
        )

    def x_wait(j, slot):
        remote(
            xs.at[j, slot], xs.at[j, slot], x_send.at[j, 0, 0], x_recv.at[j, slot], {"blk": sib}
        ).wait_recv()

    def send_own(j):
        @pl.when(has_up)
        def _():
            x_line(j, chip, 0).start()

        @pl.when(has_down)
        def _():
            x_line(j, chip, 1).start()

        x_sib(j, chip).start()

    def pass_on(j):
        for s in range(1, C):
            @pl.when(chip - s >= 0)
            def _():
                x_wait(j, core * C + chip - s)

                @pl.when(has_up)
                def _():
                    x_line(j, chip - s, 0).start()

                x_sib(j, chip - s).start()

            @pl.when(chip + s < C)
            def _():
                x_wait(j, core * C + chip + s)

                @pl.when(has_down)
                def _():
                    x_line(j, chip + s, 1).start()

                x_sib(j, chip + s).start()

    def middle(acc_g, acc_u, act, pf):
        acc_g[...] = jnp.zeros_like(acc_g)
        acc_u[...] = jnp.zeros_like(acc_u)

        square = jnp.zeros((RS, 1), F32)
        for i in range(S - 1):
            a_wait(lax.rem(sect + 1 + i, S))
        for t in range(S):
            state = rs[t].astype(F32)
            square = square + jnp.sum(state * state, axis=1, keepdims=True)
        inv = lax.rsqrt(square / (S * KC) + 1e-5)
        for i in range(S):
            t = order(i)
            xs[t, me] = (rs[t].astype(F32) * inv * gain_ref[t]).astype(BF16)
            if i < 2:
                send_own(t)

        @pl.loop(0, S)
        def _(i):
            j = order(i)
            pass_on(j)

            @pl.when(i + 2 < S)
            def _():
                send_own(order(i + 2))

            for c in range(C):
                x_wait(j, (1 - core) * C + c)
            weight_copy(i, 0).wait()
            weight_copy(i, 1).wait()
            chunk = xs[j].reshape(B * RS, KC)

            @pl.loop(0, FFL // NT)
            def _(n):
                cols = pl.ds(pl.multiple_of(n * NT, NT), NT)
                acc_g[:, cols] += jnp.dot(chunk, wg[j, :, cols], preferred_element_type=F32)
                acc_u[:, cols] += jnp.dot(chunk, wu[j, :, cols], preferred_element_type=F32)

        @pl.loop(0, FFL // NT)
        def _(n):
            cols = pl.ds(pl.multiple_of(n * NT, NT), NT)
            gate = acc_g[:, cols]
            act[:, cols] = (gate / (1.0 + jnp.exp(-gate)) * acc_u[:, cols]).astype(BF16)

        def s_copy(j):
            return remote(ss.at[j], sr.at[j], s_send.at[j], s_recv.at[j], {"blk": sib})

        def u_copy(j, d):
            return remote(sb.at[j, d], ru.at[j, d], l_send.at[j, d], u_recv.at[j, d], {"blk": up})

        def d_copy(j, d):
            return remote(sb.at[j, d], rd.at[j, d], l_send.at[j, d], d_recv.at[j, d], {"blk": down})

        def o_copy(j):
            return remote(fo.at[j], ob.at[sect], o_send.at[j], o_recv.at[sect], {"sect": j})

        def project(i):
            j = order(i)
            p = lax.rem(i, 2)
            weight_copy(i, 2).wait()

            @pl.loop(0, KC // NK)
            def _(n):
                cols = pl.ds(pl.multiple_of(n * NK, NK), NK)
                part = jnp.dot(act[...], wd[j, :, cols], preferred_element_type=F32)
                pf[p, :, :, :, cols] = part.reshape(2, C, RS, NK)

            ss[j] = pf[p, 1 - core].astype(BF16)
            s_copy(j).start()

        def stage(i):
            j = order(i)
            p = lax.rem(i, 2)
            s_copy(j).wait_recv()

            def ups():
                for e in range(C - 1):
                    d = C - 1 - e

                    @pl.when(d > chip)
                    def _():
                        mine = pf[p, core, d] + sr[j, d].astype(F32)

                        @pl.when(has_down)
                        def _():
                            u_copy(j, d).wait_recv()
                            sb[j, d] = (mine + ru[j, d].astype(F32)).astype(BF16)

                        @pl.when(jnp.logical_not(has_down))
                        def _():
                            sb[j, d] = mine.astype(BF16)

                        u_copy(j, d).start()

            def downs():
                for d in range(C - 1):
                    @pl.when(d < chip)
                    def _():
                        mine = pf[p, core, d] + sr[j, d].astype(F32)

                        @pl.when(has_up)
                        def _():
                            d_copy(j, d).wait_recv()
                            sb[j, d] = (mine + rd[j, d].astype(F32)).astype(BF16)

                        @pl.when(jnp.logical_not(has_up))
                        def _():
                            sb[j, d] = mine.astype(BF16)

                        d_copy(j, d).start()

            @pl.when(2 * chip < C)
            def _():
                ups()
                downs()

            @pl.when(2 * chip >= C)
            def _():
                downs()
                ups()

            own[j] = pf[p, core, chip] + sr[j, chip].astype(F32) + rs[j].astype(F32)

        def finish(i):
            j = order(i)

            @pl.when(has_down)
            def _():
                u_copy(j, chip).wait_recv()
                own[j] += ru[j, chip].astype(F32)

            @pl.when(has_up)
            def _():
                d_copy(j, chip).wait_recv()
                own[j] += rd[j, chip].astype(F32)

            @pl.when(i < S - 1)
            def _():
                fo[j] = own[j].astype(BF16)
                o_copy(j).start()

            @pl.when(i == S - 1)
            def _():
                ob[j] = own[j].astype(BF16)

        @pl.loop(0, S + 2)
        def _(i):
            @pl.when(i < S)
            def _():
                project(i)

            @pl.when((i >= 1) & (i <= S))
            def _():
                stage(i - 1)

            @pl.when(i >= 2)
            def _():
                finish(i - 2)

        for i in range(S - 1):
            a_copy(order(i)).wait_send()
            o_copy(order(i)).wait_send()

        @pl.loop(0, S)
        def _(j):
            s_copy(j).wait_send()
            for c in range(C):
                x_sib(j, c).wait_send()

                @pl.when((c <= chip) & has_up)
                def _():
                    x_line(j, c, 0).wait_send()

                @pl.when((c >= chip) & has_down)
                def _():
                    x_line(j, c, 1).wait_send()

                @pl.when(c != chip)
                def _():
                    u_copy(j, c).wait_send()

        for i in range(S - 1):
            t = order(i)
            remote(fo.at[t], ob.at[t], o_send.at[t], o_recv.at[t], {"sect": t}).wait_recv()
        for t in range(S):
            out_ref[t * RS:(t + 1) * RS, :] = ob[t]

    pl.run_scoped(
        middle,
        pltpu.VMEM((B * RS, FFL), F32),
        pltpu.VMEM((B * RS, FFL), F32),
        pltpu.VMEM((B * RS, FFL), BF16),
        pltpu.VMEM((2, 2, C, RS, KC), F32),
    )


def body(S, B, queries, kv_cache, lengths, resid_in, norm_gain, w_gate, w_up, w_down):
    C = B // 2
    rows, KC = queries.shape
    RS = rows // S
    ffl = w_gate.shape[1]
    dma = pltpu.SemaphoreType.DMA
    vmem = pl.BlockSpec(memory_space=pltpu.VMEM)
    hbm = pl.BlockSpec(memory_space=pl.ANY)
    return pl.pallas_call(
        functools.partial(kernel, S, C),
        out_shape=jax.ShapeDtypeStruct((rows, KC), BF16),
        in_specs=[vmem, hbm, vmem, vmem, vmem, hbm, hbm, hbm],
        out_specs=vmem,
        scratch_shapes=[
            pltpu.VMEM((S, KC, ffl), BF16),
            pltpu.VMEM((S, KC, ffl), BF16),
            pltpu.VMEM((S, ffl, KC), BF16),
            pltpu.VMEM((S, RS, KC), BF16),
            pltpu.VMEM((S, RS, KC), BF16),
            pltpu.VMEM((S, B, RS, KC), BF16),
            pltpu.VMEM((S, C, RS, KC), BF16),
            pltpu.VMEM((S, C, RS, KC), BF16),
            pltpu.VMEM((S, C, RS, KC), BF16),
            pltpu.VMEM((S, C, RS, KC), BF16),
            pltpu.VMEM((S, C, RS, KC), BF16),
            pltpu.VMEM((S, RS, KC), F32),
            pltpu.VMEM((S, RS, KC), BF16),
            pltpu.VMEM((S, RS, KC), BF16),
            dma((S,)),
            dma((3, S)),
            dma((S,)),
            dma((S,)),
            dma((S, C, 3)),
            dma((S, B)),
            dma((S,)),
            dma((S,)),
            dma((S, C)),
            dma((S, C)),
            dma((S, C)),
            dma((S,)),
            dma((S,)),
        ],
        compiler_params=pltpu.CompilerParams(
            collective_id=0, has_side_effects=True, vmem_limit_bytes=63 * 1024 * 1024
        ),
    )(
        queries, kv_cache, lengths.reshape(rows, 1), resid_in,
        norm_gain.reshape(S, 1, KC), w_gate, w_up, w_down,
    )


def solution(mesh):
    placed = (
        P("blk", "sect"),
        P("blk", None, "sect"),
        P("blk"),
        P("blk", "sect"),
        P(),
        P(None, "blk"),
        P(None, "blk"),
        P("blk", None),
    )
    return jax.shard_map(
        functools.partial(body, mesh.shape["sect"], mesh.shape["blk"]),
        mesh=mesh, in_specs=placed, out_specs=P("blk", "sect"), check_vma=False,
    )
```

time: 171 us -> 85 us (0.50)
  Pallas kernels: 0 us -> 81.8 us
  waiting for transfers between devices: 78.4 us -> 0 us
  matrix products: 35.2 us -> 0 us
  blocking collectives: 19.9 us -> 0 us
  local copies, waits for them, and re-layouts: 20.7 us -> 3.06 us
  between operations: 13.5 us -> 0.01 us
  other arithmetic: 2.27 us -> 0 us
    pallas_call x0 -> x1, Pallas kernels: none -> 81.8 us  [body(): pl.pallas_call(functools.partial(kernel, S, C), out_shape=jax.ShapeDtypeS...]
    reduce_scatter x1 -> x0, waiting for transfers between devices: 49.7 us -> none  [feed_forward(): lax.psum_scatter(jnp.dot(act, w_down, preferred_element_type=jnp.float32)...]
    dot_general x3 -> x0, matrix products: 32.1 us -> none  [the longest x1 20.2 us: feed_forward(): jnp.dot(act, w_down, preferred_element_type=jnp.float32)]
    all_gather x1 -> x0, waiting for transfers between devices: 28.7 us -> none  [feed_forward(): piece = lax.all_gather(normed, 'blk', axis=0, tiled=True)]
    all_to_all x2 -> x0, blocking collectives: 19.9 us -> none  [the longest x1 10.7 us: body(): lax.all_to_all(hidden_state, 'sect', split_axis=0, concat_axis=1, tiled=T...]
    unnamed x16 -> x1, local copies, waits for them, and re-layouts: 16.2 us -> 1.67 us
    slice x1 -> x0, local copies, waits for them, and re-layouts: 4 us -> none  [attention(): keys = cache[:, :, :, 0, :]]
    sub x1 -> x0, matrix products: 3.17 us -> none  [attention(): expo = jnp.where(live, jnp.exp(scores - top), jnp.float32(0.0))]
  transfers between devices with their start and end apart: 2 -> 0, of which waited for: 2 -> 0; matrix products, arithmetic and copies ran while one was open for 0% -> 0% of each run, Pallas kernels for 0% -> 0%
where the time goes in v1:
time: 85 us; the launch traced here: 84.9 us
  Pallas kernels  81.8 us (96%)
  local copies, waits for them, and re-layouts  3.06 us (4%)
    pallas_call x1, Pallas kernels, body(): pl.pallas_call(functools.partial(kernel, S, C), out_shape=jax.ShapeDtypeS...  81.8 us

profile of v1, /device:TPU:0, one launch (start us, length us, event | category | flops | bytes accessed | tf_op | source)
XLA Modules:
  0.0 84.9 jit_solution(2924284477406786026)
XLA Ops:
  0.0 1.4 %copy.9.len_ref = s32[128,1]{1,0:T(8,128)} copy(s32[128,1]{0,1:T(1,128)} %bitcast.3) | data formatting | bytes 1024 | tf_op jit(solution)/shard_map/reshape | solution.py:433
  1.4 81.8 %shard_map.82 = bf16[128,1024]{1,0:T(8,128)(2,1)} custom-call(bf16[128,1024]{1,0:T(8,128)(2,1)} %q_ref.1, bf16[128,32,512]{2,1,0:T(8,128)(2,1)} %kv_hbm.1, s32[128,1]{1,0:T(8,128)} %copy.9.len_ref, bf16[128,1024]{1,0:T(8,128)(2,1)} %resid_ref.1, f32[4,1,1024]{2,1,0:T(1,128)} %bitcast.2, bf16[4096,1792]{1,0:T(8,128)(2,1)} %wg_hbm.1, ...), custom_call_target="tpu_custom_call" | custom-call | tf_op jit(solution)/shard_map/pallas_call | solution.py:395
  83.2 1.7 %copy.11 = bf16[128,1024]{1,0:T(8,128)(2,1)} copy(bf16[128,1024]{1,0:T(8,128)(2,1)} %shard_map.82) | data formatting | bytes 524288

commit v2 on v1

--- a/solution.py
+++ b/solution.py
@@ -19,12 +19,12 @@
     S, C,
     q_ref, kv_hbm, len_ref, resid_ref, gain_ref, wg_hbm, wu_hbm, wd_hbm,
     out_ref,
-    wg, wu, wd, hb, rs, xs, ss, sr, sb, ru, rd, own, fo, ob,
+    wg, wu, wd, hb, count, xs, ss, sr, sb, ru, rd, own, fo, ob,
     kv_sem, w_sem, a_send, a_recv, x_send, x_recv, s_send, s_recv,
     l_send, u_recv, d_recv, o_send, o_recv,
 ):
-    RS = rs.shape[1]
-    KC = rs.shape[2]
+    RS = hb.shape[1]
+    KC = hb.shape[2]
     B = 2 * C
     FFL = wg.shape[2]
     heads = kv_hbm.shape[2] // (2 * HD)
@@ -43,8 +43,11 @@
     has_down = chip > 0
     me = core * C + chip
 
+    def turn(i):
+        return lax.rem(sect + 1 + i, S)
+
     def order(i):
-        return lax.rem(sect + 1 + i, S)
+        return lax.rem(sect + 2 * S - 1 - i, S)
 
     def remote(src, dst, ssem, rsem, dev):
         return pltpu.make_async_remote_copy(
@@ -77,10 +80,67 @@
         pl.semaphore_wait(barrier, S + has_up.astype(jnp.int32) + has_down.astype(jnp.int32))
 
     def a_copy(t):
-        return remote(hb.at[t], rs.at[sect], a_send.at[t], a_recv.at[sect], {"sect": t})
+        return remote(hb.at[t], xs.at[sect, me], a_send.at[t], a_recv.at[sect], {"sect": t})
 
     def a_wait(t):
-        remote(hb.at[t], rs.at[t], a_send.at[t], a_recv.at[t], {"sect": t}).wait_recv()
+        remote(hb.at[t], xs.at[t, me], a_send.at[t], a_recv.at[t], {"sect": t}).wait_recv()
+
+    def x_line(j, c, which):
+        slot = core * C + c
+        return remote(
+            xs.at[j, slot], xs.at[j, slot], x_send.at[j, c, which], x_recv.at[j, slot],
+            {"blk": up if which == 0 else down},
+        )
+
+    def x_sib(j, c):
+        slot = core * C + c
+        return remote(
+            xs.at[j, slot], xs.at[j, slot], x_send.at[j, c, 2], x_recv.at[j, slot], {"blk": sib}
+        )
+
+    def x_wait(j, slot):
+        remote(
+            xs.at[j, slot], xs.at[j, slot], x_send.at[j, 0, 0], x_recv.at[j, slot], {"blk": sib}
+        ).wait_recv()
+
+    def send_own(j):
+        @pl.when(has_up)
+        def _():
+            x_line(j, chip, 0).start()
+
+        @pl.when(has_down)
+        def _():
+            x_line(j, chip, 1).start()
+
+        x_sib(j, chip).start()
+
+    def pass_on(i, s):
+        j = order(i)
+
+        @pl.when(chip - s >= 0)
+        def _():
+            x_wait(j, core * C + chip - s)
+
+            @pl.when(has_up)
+            def _():
+                x_line(j, chip - s, 0).start()
+
+            x_sib(j, chip - s).start()
+
+        @pl.when(chip + s < C)
+        def _():
+            x_wait(j, core * C + chip + s)
+
+            @pl.when(has_down)
+            def _():
+                x_line(j, chip + s, 1).start()
+
+            x_sib(j, chip + s).start()
+
+    def pass_due(tick, s):
+        @pl.when((tick - s >= 0) & (tick - s < S))
+        def _():
+            pass_on(tick - s, s)
 
     def front(kv):
         def kv_copy(t):
@@ -88,22 +148,22 @@
             return pltpu.make_async_copy(kv_hbm.at[rows], kv.at[t], kv_sem.at[t])
 
         for i in range(S):
-            kv_copy(order(i)).start()
+            kv_copy(turn(i)).start()
         for i in range(S):
             weight_copy(i, 0).start()
             weight_copy(i, 1).start()
         for i in range(S):
             weight_copy(i, 2).start()
 
-        def attend(t, dst, slot):
+        def attend(t):
             kv_copy(t).wait()
             for g in range(RS // TILE):
                 rows = pl.ds(pl.multiple_of(t * RS + g * TILE, TILE), TILE)
-                count = jnp.concatenate([len_ref[rows, :]] * GROUP, axis=0)
+                ends = jnp.concatenate([count[rows, 0:1]] * GROUP, axis=0)
                 shape = (GROUP * TILE, TILE * slots)
                 row = lax.rem(lax.broadcasted_iota(jnp.int32, shape, 0), TILE)
                 col = lax.broadcasted_iota(jnp.int32, shape, 1) - row * slots
-                live = (col >= 0) & (col < count)
+                live = (col >= 0) & (col < ends)
                 for h in range(heads):
                     base = h * GROUP * HD
                     query = jnp.concatenate(
@@ -121,116 +181,83 @@
                     attn = jnp.dot(probs, part[:, HD:], preferred_element_type=F32)
                     for e in range(GROUP):
                         cols = slice(base + e * HD, base + (e + 1) * HD)
-                        dst[slot, g * TILE:(g + 1) * TILE, cols] = (
+                        hb[t, g * TILE:(g + 1) * TILE, cols] = (
                             resid_ref[rows, cols].astype(F32) + attn[e * TILE:(e + 1) * TILE]
                         ).astype(BF16)
 
+        rows_all = len_ref.shape[1]
+        count[...] = jnp.broadcast_to(len_ref[...], (rows_all, rows_all)).T
         greet()
 
-        @pl.loop(0, S - 1)
+        @pl.loop(0, S)
         def _(i):
-            t = order(i)
-            attend(t, hb, t)
-            a_copy(t).start()
-
-        attend(sect, rs, sect)
+            t = turn(i)
+            attend(t)
+
+            @pl.when(i < S - 1)
+            def _():
+                a_copy(t).start()
+
+            @pl.when(i > 0)
+            def _():
+                a_wait(order(i - 1))
+                send_own(order(i - 1))
+
+            @pl.when(i == S - 1)
+            def _():
+                xs[t, me] = hb[t]
+                send_own(t)
+
+            for s in range(1, C):
+                pass_due(i - 1, s)
 
     pl.run_scoped(front, pltpu.VMEM((S, RS, slots, kv_hbm.shape[2]), BF16))
 
-    def x_line(j, c, which):
-        slot = core * C + c
-        return remote(
-            xs.at[j, slot], xs.at[j, slot], x_send.at[j, c, which], x_recv.at[j, slot],
-            {"blk": up if which == 0 else down},
-        )
-
-    def x_sib(j, c):
-        slot = core * C + c
-        return remote(
-            xs.at[j, slot], xs.at[j, slot], x_send.at[j, c, 2], x_recv.at[j, slot], {"blk": sib}
-        )
-
-    def x_wait(j, slot):
-        remote(
-            xs.at[j, slot], xs.at[j, slot], x_send.at[j, 0, 0], x_recv.at[j, slot], {"blk": sib}
-        ).wait_recv()
-
-    def send_own(j):
-        @pl.when(has_up)
-        def _():
-            x_line(j, chip, 0).start()
-
-        @pl.when(has_down)
-        def _():
-            x_line(j, chip, 1).start()
-
-        x_sib(j, chip).start()
-
-    def pass_on(j):
-        for s in range(1, C):
-            @pl.when(chip - s >= 0)
-            def _():
-                x_wait(j, core * C + chip - s)
-
-                @pl.when(has_up)
-                def _():
-                    x_line(j, chip - s, 0).start()
-
-                x_sib(j, chip - s).start()
-
-            @pl.when(chip + s < C)
-            def _():
-                x_wait(j, core * C + chip + s)
-
-                @pl.when(has_down)
-                def _():
-                    x_line(j, chip + s, 1).start()
-
-                x_sib(j, chip + s).start()
-
-    def middle(acc_g, acc_u, act, pf):
+    def middle(acc_g, acc_u, act, pf, scaled, square):
         acc_g[...] = jnp.zeros_like(acc_g)
         acc_u[...] = jnp.zeros_like(acc_u)
-
-        square = jnp.zeros((RS, 1), F32)
-        for i in range(S - 1):
-            a_wait(lax.rem(sect + 1 + i, S))
-        for t in range(S):
-            state = rs[t].astype(F32)
-            square = square + jnp.sum(state * state, axis=1, keepdims=True)
-        inv = lax.rsqrt(square / (S * KC) + 1e-5)
-        for i in range(S):
-            t = order(i)
-            xs[t, me] = (rs[t].astype(F32) * inv * gain_ref[t]).astype(BF16)
-            if i < 2:
-                send_own(t)
+        square[...] = jnp.zeros_like(square)
+        for tick in range(S - 1, max(S, C)):
+            for s in range(1, C):
+                pass_due(tick, s)
 
         @pl.loop(0, S)
         def _(i):
             j = order(i)
-            pass_on(j)
-
-            @pl.when(i + 2 < S)
-            def _():
-                send_own(order(i + 2))
-
             for c in range(C):
                 x_wait(j, (1 - core) * C + c)
+            for b in range(B):
+                state = xs[j, b].astype(F32)
+                rows = slice(b * RS, (b + 1) * RS)
+                scaled[rows, :] = (state * gain_ref[j]).astype(BF16)
+                state = state * state
+                part = state[:, :HD]
+                for e in range(1, KC // HD):
+                    part = part + state[:, e * HD:(e + 1) * HD]
+                square[rows, :] += part
             weight_copy(i, 0).wait()
             weight_copy(i, 1).wait()
-            chunk = xs[j].reshape(B * RS, KC)
 
             @pl.loop(0, FFL // NT)
             def _(n):
                 cols = pl.ds(pl.multiple_of(n * NT, NT), NT)
-                acc_g[:, cols] += jnp.dot(chunk, wg[j, :, cols], preferred_element_type=F32)
-                acc_u[:, cols] += jnp.dot(chunk, wu[j, :, cols], preferred_element_type=F32)
+                acc_g[:, cols] += jnp.dot(scaled[...], wg[j, :, cols], preferred_element_type=F32)
+                acc_u[:, cols] += jnp.dot(scaled[...], wu[j, :, cols], preferred_element_type=F32)
+                for s in range(1, C):
+                    @pl.when(n == min(s, FFL // NT - 1))
+                    def _():
+                        pass_due(max(S, C) + i, s)
+
+        square[:, 0:1] = lax.rsqrt(
+            jnp.sum(square[...], axis=1, keepdims=True) / (S * KC) + 1e-5
+        )
 
         @pl.loop(0, FFL // NT)
         def _(n):
             cols = pl.ds(pl.multiple_of(n * NT, NT), NT)
-            gate = acc_g[:, cols]
-            act[:, cols] = (gate / (1.0 + jnp.exp(-gate)) * acc_u[:, cols]).astype(BF16)
+            inv = square[:, 0:1]
+            gate = acc_g[:, cols] * inv
+            act[:, cols] = (gate / (1.0 + jnp.exp(-gate)) * (acc_u[:, cols] * inv)).astype(BF16)
 
         def s_copy(j):
             return remote(ss.at[j], sr.at[j], s_send.at[j], s_recv.at[j], {"blk": sib})
@@ -309,7 +336,7 @@
                 downs()
                 ups()
 
-            own[j] = pf[p, core, chip] + sr[j, chip].astype(F32) + rs[j].astype(F32)
+            own[j] = pf[p, core, chip] + sr[j, chip].astype(F32) + xs[j, me].astype(F32)
 
         def finish(i):
             j = order(i)
@@ -333,7 +360,7 @@
             def _():
                 ob[j] = own[j].astype(BF16)
 
-        @pl.loop(0, S + 2)
+        @pl.loop(0, S + 3)
         def _(i):
             @pl.when(i < S)
             def _():
@@ -343,12 +370,12 @@
             def _():
                 stage(i - 1)
 
-            @pl.when(i >= 2)
-            def _():
-                finish(i - 2)
+            @pl.when(i >= 3)
+            def _():
+                finish(i - 3)
 
         for i in range(S - 1):
-            a_copy(order(i)).wait_send()
+            a_copy(turn(i)).wait_send()
             o_copy(order(i)).wait_send()
 
         @pl.loop(0, S)
@@ -381,6 +408,8 @@
         pltpu.VMEM((B * RS, FFL), F32),
         pltpu.VMEM((B * RS, FFL), BF16),
         pltpu.VMEM((2, 2, C, RS, KC), F32),
+        pltpu.VMEM((B * RS, KC), BF16),
+        pltpu.VMEM((B * RS, HD), F32),
     )
 
 
@@ -402,7 +431,7 @@
             pltpu.VMEM((S, KC, ffl), BF16),
             pltpu.VMEM((S, ffl, KC), BF16),
             pltpu.VMEM((S, RS, KC), BF16),
-            pltpu.VMEM((S, RS, KC), BF16),
+            pltpu.VMEM((rows, rows), jnp.int32),
             pltpu.VMEM((S, B, RS, KC), BF16),
             pltpu.VMEM((S, C, RS, KC), BF16),
             pltpu.VMEM((S, C, RS, KC), BF16),
@@ -430,7 +459,7 @@
             collective_id=0, has_side_effects=True, vmem_limit_bytes=63 * 1024 * 1024
         ),
     )(
-        queries, kv_cache, lengths.reshape(rows, 1), resid_in,
+        queries, kv_cache, lengths.reshape(1, rows), resid_in,
         norm_gain.reshape(S, 1, KC), w_gate, w_up, w_down,
     )
 

time: 85 us -> 73 us (0.86)
  Pallas kernels: 81.8 us -> 71.2 us
  local copies, waits for them, and re-layouts: 3.06 us -> 1.67 us
    pallas_call x1, Pallas kernels: 81.8 us -> 71.2 us  [body(): pl.pallas_call(functools.partial(kernel, S, C), out_shape=jax.ShapeDtypeS...]
    reshape x1 -> x0, local copies, waits for them, and re-layouts: 1.39 us -> none  [body(): lengths.reshape(rows, 1)]
where the time goes in v2:
time: 73 us; the launch traced here: 72.8 us
  Pallas kernels  71.2 us (98%)
  local copies, waits for them, and re-layouts  1.67 us (2%)
    pallas_call x1, Pallas kernels, body(): pl.pallas_call(functools.partial(kernel, S, C), out_shape=jax.ShapeDtypeS...  71.2 us
    unnamed x1, local copies, waits for them, and re-layouts  1.67 us

profile of v2, /device:TPU:0, one launch (start us, length us, event | category | flops | bytes accessed | tf_op | source)
XLA Modules:
  0.0 72.8 jit_solution(3335859046601972642)
XLA Ops:
  0.0 71.2 %shard_map.82 = bf16[128,1024]{1,0:T(8,128)(2,1)} custom-call(bf16[128,1024]{1,0:T(8,128)(2,1)} %q_ref.1, bf16[128,32,512]{2,1,0:T(8,128)(2,1)} %kv_hbm.1, s32[1,128]{1,0:T(1,128)} %bitcast.3, bf16[128,1024]{1,0:T(8,128)(2,1)} %resid_ref.1, f32[4,1,1024]{2,1,0:T(1,128)} %bitcast.2, bf16[4096,1792]{1,0:T(8,128)(2,1)} %wg_hbm.1, bf16[4096,1792]{1,0:T(8,128)(2,1)} %wu_hbm.1, ...), custom_call_target="tpu_custom_call" | custom-call | tf_op jit(solution)/shard_map/pallas_call | solution.py:424
  71.2 1.7 %copy.10 = bf16[128,1024]{1,0:T(8,128)(2,1)} copy(bf16[128,1024]{1,0:T(8,128)(2,1)} %shard_map.82) | data formatting | bytes 524288

commit v3 on v2

--- a/solution.py
+++ b/solution.py
@@ -13,6 +13,10 @@
 MESH = pl.DeviceIdType.MESH
 F32 = jnp.float32
 BF16 = jnp.bfloat16
+
+
+def widest(total, most):
+    return max(w for w in range(128, most + 1, 128) if total % w == 0)
 
 
 def kernel(
@@ -29,8 +33,8 @@
     FFL = wg.shape[2]
     heads = kv_hbm.shape[2] // (2 * HD)
     slots = kv_hbm.shape[1]
-    NT = 256 if FFL % 256 == 0 else 128
-    NK = 256 if KC % 256 == 0 else 128
+    NT = widest(FFL, 1024)
+    NK = widest(KC, 512)
 
     sect = lax.axis_index("sect")
     blk = lax.axis_index("blk")
@@ -149,12 +153,6 @@
 
         for i in range(S):
             kv_copy(turn(i)).start()
-        for i in range(S):
-            weight_copy(i, 0).start()
-            weight_copy(i, 1).start()
-        for i in range(S):
-            weight_copy(i, 2).start()
-
         def attend(t):
             kv_copy(t).wait()
             for g in range(RS // TILE):
@@ -177,7 +175,7 @@
                     scores = jnp.where(live, scores, -1e30)
                     top = jnp.max(scores, axis=1, keepdims=True)
                     expo = jnp.where(live, jnp.exp(scores - top), 0.0)
-                    probs = (expo / jnp.sum(expo, axis=1, keepdims=True)).astype(BF16)
+                    probs = (expo * (1.0 / jnp.sum(expo, axis=1, keepdims=True))).astype(BF16)
                     attn = jnp.dot(probs, part[:, HD:], preferred_element_type=F32)
                     for e in range(GROUP):
                         cols = slice(base + e * HD, base + (e + 1) * HD)
@@ -197,6 +195,11 @@
             @pl.when(i < S - 1)
             def _():
                 a_copy(t).start()
+
+            @pl.when(i < 2)
+            def _():
+                weight_copy(i, 0).start()
+                weight_copy(i, 1).start()
 
             @pl.when(i > 0)
             def _():
@@ -238,13 +241,20 @@
             weight_copy(i, 0).wait()
             weight_copy(i, 1).wait()
 
+            @pl.when(i + 2 < S)
+            def _():
+                weight_copy(i + 2, 0).start()
+                weight_copy(i + 2, 1).start()
+
+            weight_copy(i, 2).start()
+
             @pl.loop(0, FFL // NT)
             def _(n):
                 cols = pl.ds(pl.multiple_of(n * NT, NT), NT)
                 acc_g[:, cols] += jnp.dot(scaled[...], wg[j, :, cols], preferred_element_type=F32)
                 acc_u[:, cols] += jnp.dot(scaled[...], wu[j, :, cols], preferred_element_type=F32)
                 for s in range(1, C):
-                    @pl.when(n == min(s, FFL // NT - 1))
+                    @pl.when(n == min(s - 1, FFL // NT - 1))
                     def _():
                         pass_due(max(S, C) + i, s)
 

time: 73 us -> 72.3 us (level)
  no operation moved by 1% of the time
where the time goes in v3:
time: 72.3 us; the launch traced here: 72.2 us
  Pallas kernels  70.5 us (98%)
  local copies, waits for them, and re-layouts  1.67 us (2%)
    pallas_call x1, Pallas kernels, body(): pl.pallas_call(functools.partial(kernel, S, C), out_shape=jax.ShapeDtypeS...  70.5 us
    unnamed x1, local copies, waits for them, and re-layouts  1.67 us

profile of v3, /device:TPU:0, one launch (start us, length us, event | category | flops | bytes accessed | tf_op | source)
XLA Modules:
  0.0 72.2 jit_solution(12154796284685164241)
XLA Ops:
  0.0 70.5 %shard_map.82 = bf16[128,1024]{1,0:T(8,128)(2,1)} custom-call(bf16[128,1024]{1,0:T(8,128)(2,1)} %q_ref.1, bf16[128,32,512]{2,1,0:T(8,128)(2,1)} %kv_hbm.1, s32[1,128]{1,0:T(1,128)} %bitcast.3, bf16[128,1024]{1,0:T(8,128)(2,1)} %resid_ref.1, f32[4,1,1024]{2,1,0:T(1,128)} %bitcast.2, bf16[4096,1792]{1,0:T(8,128)(2,1)} %wg_hbm.1, bf16[4096,1792]{1,0:T(8,128)(2,1)} %wu_hbm.1, ...), custom_call_target="tpu_custom_call" | custom-call | tf_op jit(solution)/shard_map/pallas_call | solution.py:434
  70.5 1.7 %copy.10 = bf16[128,1024]{1,0:T(8,128)(2,1)} copy(bf16[128,1024]{1,0:T(8,128)(2,1)} %shard_map.82) | data formatting | bytes 524288

commit v4 on v3

--- a/solution.py
+++ b/solution.py
@@ -30,6 +30,9 @@
     RS = hb.shape[1]
     KC = hb.shape[2]
     B = 2 * C
+    RH = xs.shape[2]
+    H = RS // RH
+    V = H * S
     FFL = wg.shape[2]
     heads = kv_hbm.shape[2] // (2 * HD)
     slots = kv_hbm.shape[1]
@@ -53,6 +56,9 @@
     def order(i):
         return lax.rem(sect + 2 * S - 1 - i, S)
 
+    def place(v):
+        return (v // S) * S + order(lax.rem(v, S))
+
     def remote(src, dst, ssem, rsem, dev):
         return pltpu.make_async_remote_copy(
             src_ref=src, dst_ref=dst, send_sem=ssem, recv_sem=rsem,
@@ -83,11 +89,14 @@
 
         pl.semaphore_wait(barrier, S + has_up.astype(jnp.int32) + has_down.astype(jnp.int32))
 
-    def a_copy(t):
-        return remote(hb.at[t], xs.at[sect, me], a_send.at[t], a_recv.at[sect], {"sect": t})
-
-    def a_wait(t):
-        remote(hb.at[t], xs.at[t, me], a_send.at[t], a_recv.at[t], {"sect": t}).wait_recv()
+    def a_copy(h, t):
+        return remote(
+            hb.at[t, pl.ds(h * RH, RH)], xs.at[h * S + sect, me],
+            a_send.at[h * S + t], a_recv.at[h * S + sect], {"sect": t},
+        )
+
+    def a_wait(j):
+        remote(xs.at[j, me], xs.at[j, me], a_send.at[0], a_recv.at[j], {"blk": sib}).wait_recv()
 
     def x_line(j, c, which):
         slot = core * C + c
@@ -118,8 +127,8 @@
 
         x_sib(j, chip).start()
 
-    def pass_on(i, s):
-        j = order(i)
+    def pass_on(v, s):
+        j = place(v)
 
         @pl.when(chip - s >= 0)
         def _():
@@ -142,9 +151,18 @@
             x_sib(j, chip + s).start()
 
     def pass_due(tick, s):
-        @pl.when((tick - s >= 0) & (tick - s < S))
+        @pl.when((tick - s >= 0) & (tick - s < V))
         def _():
             pass_on(tick - s, s)
+
+    def own_due(tick):
+        @pl.when((tick >= 0) & (tick < V))
+        def _():
+            @pl.when(lax.rem(tick + S, S) < S - 1)
+            def _():
+                a_wait(place(tick))
+
+            send_own(place(tick))
 
     def front(kv):
         def kv_copy(t):
@@ -194,80 +212,94 @@
 
             @pl.when(i < S - 1)
             def _():
-                a_copy(t).start()
+                for h in range(H):
+                    a_copy(h, t).start()
 
             @pl.when(i < 2)
             def _():
                 weight_copy(i, 0).start()
                 weight_copy(i, 1).start()
 
-            @pl.when(i > 0)
-            def _():
-                a_wait(order(i - 1))
-                send_own(order(i - 1))
-
             @pl.when(i == S - 1)
             def _():
-                xs[t, me] = hb[t]
-                send_own(t)
-
+                for h in range(H):
+                    xs[h * S + t, me] = hb[t, h * RH:(h + 1) * RH]
+
+            own_due(i - 1)
             for s in range(1, C):
                 pass_due(i - 1, s)
 
     pl.run_scoped(front, pltpu.VMEM((S, RS, slots, kv_hbm.shape[2]), BF16))
 
     def middle(acc_g, acc_u, act, pf, scaled, square):
-        acc_g[...] = jnp.zeros_like(acc_g)
-        acc_u[...] = jnp.zeros_like(acc_u)
-        square[...] = jnp.zeros_like(square)
         for tick in range(S - 1, max(S, C)):
+            own_due(tick)
             for s in range(1, C):
                 pass_due(tick, s)
 
-        @pl.loop(0, S)
-        def _(i):
-            j = order(i)
+        def expand(v):
+            i = lax.rem(v, S)
+            t = order(i)
+            j = place(v)
+
+            @pl.when(i == 0)
+            def _():
+                acc_g[...] = jnp.zeros_like(acc_g)
+                acc_u[...] = jnp.zeros_like(acc_u)
+                square[...] = jnp.zeros_like(square)
+
+            own_due(max(S, C) + v)
             for c in range(C):
                 x_wait(j, (1 - core) * C + c)
             for b in range(B):
                 state = xs[j, b].astype(F32)
-                rows = slice(b * RS, (b + 1) * RS)
-                scaled[rows, :] = (state * gain_ref[j]).astype(BF16)
+                rows = slice(b * RH, (b + 1) * RH)
+                scaled[rows, :] = (state * gain_ref[t]).astype(BF16)
                 state = state * state
                 part = state[:, :HD]
                 for e in range(1, KC // HD):
                     part = part + state[:, e * HD:(e + 1) * HD]
                 square[rows, :] += part
-            weight_copy(i, 0).wait()
-            weight_copy(i, 1).wait()
-
-            @pl.when(i + 2 < S)
-            def _():
-                weight_copy(i + 2, 0).start()
-                weight_copy(i + 2, 1).start()
-
-            weight_copy(i, 2).start()
+
+            @pl.when(v < S)
+            def _():
+                weight_copy(i, 0).wait()
+                weight_copy(i, 1).wait()
+
+                @pl.when(i + 2 < S)
+                def _():
+                    weight_copy(i + 2, 0).start()
+                    weight_copy(i + 2, 1).start()
+
+                weight_copy(i, 2).start()
 
             @pl.loop(0, FFL // NT)
             def _(n):
                 cols = pl.ds(pl.multiple_of(n * NT, NT), NT)
-                acc_g[:, cols] += jnp.dot(scaled[...], wg[j, :, cols], preferred_element_type=F32)
-                acc_u[:, cols] += jnp.dot(scaled[...], wu[j, :, cols], preferred_element_type=F32)
+                acc_g[:, cols] += jnp.dot(scaled[...], wg[t, :, cols], preferred_element_type=F32)
+                acc_u[:, cols] += jnp.dot(scaled[...], wu[t, :, cols], preferred_element_type=F32)
                 for s in range(1, C):
                     @pl.when(n == min(s - 1, FFL // NT - 1))
                     def _():
-                        pass_due(max(S, C) + i, s)
-
-        square[:, 0:1] = lax.rsqrt(
-            jnp.sum(square[...], axis=1, keepdims=True) / (S * KC) + 1e-5
-        )
-
-        @pl.loop(0, FFL // NT)
-        def _(n):
-            cols = pl.ds(pl.multiple_of(n * NT, NT), NT)
-            inv = square[:, 0:1]
-            gate = acc_g[:, cols] * inv
-            act[:, cols] = (gate / (1.0 + jnp.exp(-gate)) * (acc_u[:, cols] * inv)).astype(BF16)
+                        pass_due(max(S, C) + v, s)
+
+        def activate():
+            square[:, 0:1] = lax.rsqrt(
+                jnp.sum(square[...], axis=1, keepdims=True) / (S * KC) + 1e-5
+            )
+
+            @pl.loop(0, FFL // 128)
+            def _(n):
+                cols = pl.ds(pl.multiple_of(n * 128, 128), 128)
+                inv = square[:, 0:1]
+                gate = acc_g[:, cols] * inv
+                act[:, cols] = (gate / (1.0 + jnp.exp(-gate)) * (acc_u[:, cols] * inv)).astype(BF16)
+
+        @pl.loop(0, S)
+        def _(v):
+            expand(v)
+
+        activate()
 
         def s_copy(j):
             return remote(ss.at[j], sr.at[j], s_send.at[j], s_recv.at[j], {"blk": sib})
@@ -279,25 +311,32 @@
             return remote(sb.at[j, d], rd.at[j, d], l_send.at[j, d], d_recv.at[j, d], {"blk": down})
 
         def o_copy(j):
-            return remote(fo.at[j], ob.at[sect], o_send.at[j], o_recv.at[sect], {"sect": j})
-
-        def project(i):
-            j = order(i)
-            p = lax.rem(i, 2)
-            weight_copy(i, 2).wait()
+            there = (j // S) * S + sect
+            return remote(
+                fo.at[j], ob.at[there], o_send.at[j], o_recv.at[there], {"sect": lax.rem(j, S)}
+            )
+
+        def project(v):
+            j = place(v)
+            t = lax.rem(j, S)
+            p = lax.rem(v, 2)
+
+            @pl.when(v < S)
+            def _():
+                weight_copy(v, 2).wait()
 
             @pl.loop(0, KC // NK)
             def _(n):
                 cols = pl.ds(pl.multiple_of(n * NK, NK), NK)
-                part = jnp.dot(act[...], wd[j, :, cols], preferred_element_type=F32)
-                pf[p, :, :, :, cols] = part.reshape(2, C, RS, NK)
+                part = jnp.dot(act[...], wd[t, :, cols], preferred_element_type=F32)
+                pf[p, :, :, :, cols] = part.reshape(2, C, RH, NK)
 
             ss[j] = pf[p, 1 - core].astype(BF16)
             s_copy(j).start()
 
-        def stage(i):
-            j = order(i)
-            p = lax.rem(i, 2)
+        def stage(v):
+            j = place(v)
+            p = lax.rem(v, 2)
             s_copy(j).wait_recv()
 
             def ups():
@@ -348,8 +387,9 @@
 
             own[j] = pf[p, core, chip] + sr[j, chip].astype(F32) + xs[j, me].astype(F32)
 
-        def finish(i):
-            j = order(i)
+        def finish(v):
+            j = place(v)
+            i = lax.rem(v, S)
 
             @pl.when(has_down)
             def _():
@@ -370,25 +410,36 @@
             def _():
                 ob[j] = own[j].astype(BF16)
 
-        @pl.loop(0, S + 3)
-        def _(i):
-            @pl.when(i < S)
-            def _():
-                project(i)
-
-            @pl.when((i >= 1) & (i <= S))
-            def _():
-                stage(i - 1)
-
-            @pl.when(i >= 3)
-            def _():
-                finish(i - 3)
-
-        for i in range(S - 1):
-            a_copy(turn(i)).wait_send()
-            o_copy(order(i)).wait_send()
-
-        @pl.loop(0, S)
+        @pl.loop(0, V + 3)
+        def _(v):
+            if H > 1:
+                @pl.when((v > 0) & (v < V) & (lax.rem(v, S) == 0))
+                def _():
+                    activate()
+
+            @pl.when(v < V)
+            def _():
+                project(v)
+
+            @pl.when((v >= 1) & (v <= V))
+            def _():
+                stage(v - 1)
+
+            @pl.when(v >= 3)
+            def _():
+                finish(v - 3)
+
+            if H > 1:
+                @pl.when(v + S < V)
+                def _():
+                    expand(v + S)
+
+        for h in range(H):
+            for i in range(S - 1):
+                a_copy(h, turn(i)).wait_send()
+                o_copy(h * S + order(i)).wait_send()
+
+        @pl.loop(0, V)
         def _(j):
             s_copy(j).wait_send()
             for c in range(C):
@@ -406,20 +457,24 @@
                 def _():
                     u_copy(j, c).wait_send()
 
-        for i in range(S - 1):
-            t = order(i)
-            remote(fo.at[t], ob.at[t], o_send.at[t], o_recv.at[t], {"sect": t}).wait_recv()
+        for h in range(H):
+            for i in range(S - 1):
+                j = h * S + order(i)
+                remote(
+                    fo.at[j], ob.at[j], o_send.at[j], o_recv.at[j], {"sect": order(i)}
+                ).wait_recv()
         for t in range(S):
-            out_ref[t * RS:(t + 1) * RS, :] = ob[t]
+            for h in range(H):
+                out_ref[t * RS + h * RH:t * RS + (h + 1) * RH, :] = ob[h * S + t]
 
     pl.run_scoped(
         middle,
-        pltpu.VMEM((B * RS, FFL), F32),
-        pltpu.VMEM((B * RS, FFL), F32),
-        pltpu.VMEM((B * RS, FFL), BF16),
-        pltpu.VMEM((2, 2, C, RS, KC), F32),
-        pltpu.VMEM((B * RS, KC), BF16),
-        pltpu.VMEM((B * RS, HD), F32),
+        pltpu.VMEM((B * RH, FFL), F32),
+        pltpu.VMEM((B * RH, FFL), F32),
+        pltpu.VMEM((B * RH, FFL), BF16),
+        pltpu.VMEM((2, 2, C, RH, KC), F32),
+        pltpu.VMEM((B * RH, KC), BF16),
+        pltpu.VMEM((B * RH, HD), F32),
     )
 
 
@@ -427,6 +482,9 @@
     C = B // 2
     rows, KC = queries.shape
     RS = rows // S
+    H = 2 if RS % (2 * TILE) == 0 else 1
+    RH = RS // H
+    V = H * S
     ffl = w_gate.shape[1]
     dma = pltpu.SemaphoreType.DMA
     vmem = pl.BlockSpec(memory_space=pltpu.VMEM)
@@ -442,28 +500,28 @@
             pltpu.VMEM((S, ffl, KC), BF16),
             pltpu.VMEM((S, RS, KC), BF16),
             pltpu.VMEM((rows, rows), jnp.int32),
-            pltpu.VMEM((S, B, RS, KC), BF16),
-            pltpu.VMEM((S, C, RS, KC), BF16),
-            pltpu.VMEM((S, C, RS, KC), BF16),
-            pltpu.VMEM((S, C, RS, KC), BF16),
-            pltpu.VMEM((S, C, RS, KC), BF16),
-            pltpu.VMEM((S, C, RS, KC), BF16),
-            pltpu.VMEM((S, RS, KC), F32),
-            pltpu.VMEM((S, RS, KC), BF16),
-            pltpu.VMEM((S, RS, KC), BF16),
+            pltpu.VMEM((V, B, RH, KC), BF16),
+            pltpu.VMEM((V, C, RH, KC), BF16),
+            pltpu.VMEM((V, C, RH, KC), BF16),
+            pltpu.VMEM((V, C, RH, KC), BF16),
+            pltpu.VMEM((V, C, RH, KC), BF16),
+            pltpu.VMEM((V, C, RH, KC), BF16),
+            pltpu.VMEM((V, RH, KC), F32),
+            pltpu.VMEM((V, RH, KC), BF16),
+            pltpu.VMEM((V, RH, KC), BF16),
             dma((S,)),
             dma((3, S)),
-            dma((S,)),
-            dma((S,)),
-            dma((S, C, 3)),
-            dma((S, B)),
-            dma((S,)),
-            dma((S,)),
-            dma((S, C)),
-            dma((S, C)),
-            dma((S, C)),
-            dma((S,)),
-            dma((S,)),
+            dma((V,)),
+            dma((V,)),
+            dma((V, C, 3)),
+            dma((V, B)),
+            dma((V,)),
+            dma((V,)),
+            dma((V, C)),
+            dma((V, C)),
+            dma((V, C)),
+            dma((V,)),
+            dma((V,)),
         ],
         compiler_params=pltpu.CompilerParams(
             collective_id=0, has_side_effects=True, vmem_limit_bytes=63 * 1024 * 1024

time: 72.3 us -> 84.6 us (1.17)
  Pallas kernels: 70.5 us -> 82.8 us
    pallas_call x1, Pallas kernels: 70.5 us -> 82.8 us  [body(): pl.pallas_call(functools.partial(kernel, S, C), out_shape=jax.ShapeDtypeS...]
where the time goes in v4:
time: 84.6 us; the launch traced here: 84.5 us
  Pallas kernels  82.8 us (98%)
  local copies, waits for them, and re-layouts  1.67 us (2%)
    pallas_call x1, Pallas kernels, body(): pl.pallas_call(functools.partial(kernel, S, C), out_shape=jax.ShapeDtypeS...  82.8 us

profile of v4, /device:TPU:0, one launch (start us, length us, event | category | flops | bytes accessed | tf_op | source)
XLA Modules:
  0.0 84.5 jit_solution(2563772348400396100)
XLA Ops:
  0.0 82.8 %shard_map.82 = bf16[128,1024]{1,0:T(8,128)(2,1)} custom-call(bf16[128,1024]{1,0:T(8,128)(2,1)} %q_ref.1, bf16[128,32,512]{2,1,0:T(8,128)(2,1)} %kv_hbm.1, s32[1,128]{1,0:T(1,128)} %bitcast.3, bf16[128,1024]{1,0:T(8,128)(2,1)} %resid_ref.1, f32[4,1,1024]{2,1,0:T(1,128)} %bitcast.2, bf16[4096,1792]{1,0:T(8,128)(2,1)} %wg_hbm.1, bf16[4096,1792]{1,0:T(8,128)(2,1)} %wu_hbm.1, ...), custom_call_target="tpu_custom_call" | custom-call | tf_op jit(solution)/shard_map/pallas_call | solution.py:492
  82.8 1.7 %copy.10 = bf16[128,1024]{1,0:T(8,128)(2,1)} copy(bf16[128,1024]{1,0:T(8,128)(2,1)} %shard_map.82) | data formatting | bytes 524288

commit v5 on v3

--- a/solution.py
+++ b/solution.py
@@ -23,9 +23,9 @@
     S, C,
     q_ref, kv_hbm, len_ref, resid_ref, gain_ref, wg_hbm, wu_hbm, wd_hbm,
     out_ref,
-    wg, wu, wd, hb, count, xs, ss, sr, sb, ru, rd, own, fo, ob,
+    wg, wu, wd, hb, count, xs, ss, sr, sb, ru, own, fo, ob,
     kv_sem, w_sem, a_send, a_recv, x_send, x_recv, s_send, s_recv,
-    l_send, u_recv, d_recv, o_send, o_recv,
+    l_send, u_recv, o_send, o_recv,
 ):
     RS = hb.shape[1]
     KC = hb.shape[2]
@@ -73,15 +73,12 @@
             )
         pl.semaphore_signal(barrier, inc=1, device_id={"blk": sib}, device_id_type=MESH)
 
-        @pl.when(has_up)
-        def _():
-            pl.semaphore_signal(barrier, inc=1, device_id={"blk": up}, device_id_type=MESH)
-
-        @pl.when(has_down)
-        def _():
-            pl.semaphore_signal(barrier, inc=1, device_id={"blk": down}, device_id_type=MESH)
-
-        pl.semaphore_wait(barrier, S + has_up.astype(jnp.int32) + has_down.astype(jnp.int32))
+        for e in range(1, C):
+            pl.semaphore_signal(
+                barrier, inc=1, device_id={"blk": lax.rem(chip + e, C) * 2 + core},
+                device_id_type=MESH,
+            )
+        pl.semaphore_wait(barrier, S + C - 1)
 
     def a_copy(t):
         return remote(hb.at[t], xs.at[sect, me], a_send.at[t], a_recv.at[sect], {"sect": t})
@@ -272,11 +269,16 @@
         def s_copy(j):
             return remote(ss.at[j], sr.at[j], s_send.at[j], s_recv.at[j], {"blk": sib})
 
-        def u_copy(j, d):
-            return remote(sb.at[j, d], ru.at[j, d], l_send.at[j, d], u_recv.at[j, d], {"blk": up})
-
-        def d_copy(j, d):
-            return remote(sb.at[j, d], rd.at[j, d], l_send.at[j, d], d_recv.at[j, d], {"blk": down})
+        def r_copy(j, d):
+            return remote(
+                sb.at[j, d], ru.at[j, chip], l_send.at[j, d], u_recv.at[j, chip],
+                {"blk": d * 2 + core},
+            )
+
+        def r_wait(j, c):
+            remote(
+                sb.at[j, c], ru.at[j, c], l_send.at[j, c], u_recv.at[j, c], {"blk": sib}
+            ).wait_recv()
 
         def o_copy(j):
             return remote(fo.at[j], ob.at[sect], o_send.at[j], o_recv.at[sect], {"sect": j})
@@ -300,66 +302,22 @@
             p = lax.rem(i, 2)
             s_copy(j).wait_recv()
 
-            def ups():
-                for e in range(C - 1):
-                    d = C - 1 - e
-
-                    @pl.when(d > chip)
+            for e in range(C - 1, 0, -1):
+                for d in (chip + e, chip - e):
+                    @pl.when((d >= 0) & (d < C))
                     def _():
-                        mine = pf[p, core, d] + sr[j, d].astype(F32)
-
-                        @pl.when(has_down)
-                        def _():
-                            u_copy(j, d).wait_recv()
-                            sb[j, d] = (mine + ru[j, d].astype(F32)).astype(BF16)
-
-                        @pl.when(jnp.logical_not(has_down))
-                        def _():
-                            sb[j, d] = mine.astype(BF16)
-
-                        u_copy(j, d).start()
-
-            def downs():
-                for d in range(C - 1):
-                    @pl.when(d < chip)
-                    def _():
-                        mine = pf[p, core, d] + sr[j, d].astype(F32)
-
-                        @pl.when(has_up)
-                        def _():
-                            d_copy(j, d).wait_recv()
-                            sb[j, d] = (mine + rd[j, d].astype(F32)).astype(BF16)
-
-                        @pl.when(jnp.logical_not(has_up))
-                        def _():
-                            sb[j, d] = mine.astype(BF16)
-
-                        d_copy(j, d).start()
-
-            @pl.when(2 * chip < C)
-            def _():
-                ups()
-                downs()
-
-            @pl.when(2 * chip >= C)
-            def _():
-                downs()
-                ups()
+                        sb[j, d] = (pf[p, core, d] + sr[j, d].astype(F32)).astype(BF16)
+                        r_copy(j, d).start()
 
             own[j] = pf[p, core, chip] + sr[j, chip].astype(F32) + xs[j, me].astype(F32)
 
         def finish(i):
             j = order(i)
 
-            @pl.when(has_down)
-            def _():
-                u_copy(j, chip).wait_recv()
-                own[j] += ru[j, chip].astype(F32)
-
-            @pl.when(has_up)
-            def _():
-                d_copy(j, chip).wait_recv()
-                own[j] += rd[j, chip].astype(F32)
+            for e in range(1, C):
+                c = lax.rem(chip + e, C)
+                r_wait(j, c)
+                own[j] += ru[j, c].astype(F32)
 
             @pl.when(i < S - 1)
             def _():
@@ -404,7 +362,7 @@
 
                 @pl.when(c != chip)
                 def _():
-                    u_copy(j, c).wait_send()
+                    r_copy(j, c).wait_send()
 
         for i in range(S - 1):
             t = order(i)
@@ -447,7 +405,6 @@
             pltpu.VMEM((S, C, RS, KC), BF16),
             pltpu.VMEM((S, C, RS, KC), BF16),
             pltpu.VMEM((S, C, RS, KC), BF16),
-            pltpu.VMEM((S, C, RS, KC), BF16),
             pltpu.VMEM((S, RS, KC), F32),
             pltpu.VMEM((S, RS, KC), BF16),
             pltpu.VMEM((S, RS, KC), BF16),
@@ -459,7 +416,6 @@
             dma((S, B)),
             dma((S,)),
             dma((S,)),
-            dma((S, C)),
             dma((S, C)),
             dma((S, C)),
             dma((S,)),

time: 72.3 us -> 66 us (0.913)
  Pallas kernels: 70.5 us -> 64.2 us
    pallas_call x1, Pallas kernels: 70.5 us -> 64.2 us  [body(): pl.pallas_call(functools.partial(kernel, S, C), out_shape=jax.ShapeDtypeS...]
where the time goes in v5:
time: 66 us; the launch traced here: 65.9 us
  Pallas kernels  64.2 us (97%)
  local copies, waits for them, and re-layouts  1.67 us (3%)
    pallas_call x1, Pallas kernels, body(): pl.pallas_call(functools.partial(kernel, S, C), out_shape=jax.ShapeDtypeS...  64.2 us
    unnamed x1, local copies, waits for them, and re-layouts  1.67 us

profile of v5, /device:TPU:0, one launch (start us, length us, event | category | flops | bytes accessed | tf_op | source)
XLA Modules:
  0.0 65.9 jit_solution(18014148101797500288)
XLA Ops:
  0.0 64.2 %shard_map.82 = bf16[128,1024]{1,0:T(8,128)(2,1)} custom-call(bf16[128,1024]{1,0:T(8,128)(2,1)} %q_ref.1, bf16[128,32,512]{2,1,0:T(8,128)(2,1)} %kv_hbm.1, s32[1,128]{1,0:T(1,128)} %bitcast.3, bf16[128,1024]{1,0:T(8,128)(2,1)} %resid_ref.1, f32[4,1,1024]{2,1,0:T(1,128)} %bitcast.2, bf16[4096,1792]{1,0:T(8,128)(2,1)} %wg_hbm.1, bf16[4096,1792]{1,0:T(8,128)(2,1)} %wu_hbm.1, ...), custom_call_target="tpu_custom_call" | custom-call | tf_op jit(solution)/shard_map/pallas_call | solution.py:392
  64.2 1.7 %copy.10 = bf16[128,1024]{1,0:T(8,128)(2,1)} copy(bf16[128,1024]{1,0:T(8,128)(2,1)} %shard_map.82) | data formatting | bytes 524288
